TPU v7x, 32 devices: a whole 2x2x4 slice. The times are simulated.
32 devices in a mesh: row: 8 (over y, x, core), col: 4 (over z).
Axes of the slice: x: 2, y: 2, z: 4, core: 2. Of those that a mesh axis runs over, the one named last changes fastest.
Arguments:
- traces: bfloat16 [4096, 782], P(('row', 'col')), may hold values from -60 to 60
- taps: float32 [16], replicated, may hold values from -1.5 to 1.5
Outputs:
- correlations: float32 [32, 4096, 4096], P(None, 'row', 'col')
All inputs are finite; a program needn't handle non-finite values.
Results may differ from a plain program's by a relative error of at most 0.0036.
Values may be sent and summed in bfloat16 or wider, within the bound.
A program may use at most 256 MiB of HBM per device.

v0:
```python
import math
import jax
import jax.numpy as jnp
from jax import lax
from jax.sharding import PartitionSpec as P

LAGS = 32


def from_root(array, axis, root):
    mine = lax.axis_index(axis) == root
    return lax.psum(jnp.where(mine, array, jnp.zeros_like(array)), axis)


def whiten(traces, taps, count):
    samples = traces.astype(jnp.float32)
    decimated = jnp.zeros((samples.shape[0], count), jnp.float32)
    for k in range(taps.shape[0]):
        decimated = decimated + taps[k] * samples[:, k : k + 2 * count - 1 : 2]
    centred = decimated - jnp.mean(decimated, axis=1, keepdims=True)
    spread = jnp.sqrt(jnp.mean(centred * centred, axis=1, keepdims=True) + 1e-06)
    return (centred / spread).astype(jnp.bfloat16)


def on_device(traces, taps):
    count = (traces.shape[1] - taps.shape[0] + 2) // 2
    factor = lax.axis_size("row") // lax.axis_size("col")
    column = lax.axis_index("col")
    source = lax.all_gather(traces, "col", axis=0, tiled=True)
    first_block = whiten(source, taps, count)
    pieces = [from_root(source, "row", factor * column + k) for k in range(factor)]
    second_block = jnp.concatenate(pieces, axis=0)
    second_block = whiten(second_block, taps, count)
    lag_count = LAGS
    width = count - lag_count + 1
    scale_factor = 1.0 / math.sqrt(width)
    left = first_block[:, :width]
    groups = []
    for group in range(lag_count // 8):
        shifted = jnp.stack(
            [second_block[:, group * 8 + lag : group * 8 + lag + width] for lag in range(8)], axis=0
        )
        product = jnp.einsum("in,ljn->lij", left, shifted, preferred_element_type=jnp.float32)
        groups.append(product * scale_factor)
    return jnp.concatenate(groups, axis=0)


def solution(mesh):
    placed = (P(("row", "col"), None), P())
    return jax.shard_map(
        on_device, mesh=mesh, in_specs=placed, out_specs=P(None, "row", "col"), check_vma=False
    )
```

profile of v0, /device:TPU:0, one launch (start us, length us, event | category | flops | bytes accessed | tf_op | source)
XLA Modules:
  0.0 332.4 jit_solution(4783237983157764529)
XLA Ops:
  6.5 20.8 %all_gather.3 = bf16[512,782]{0,1:T(8,128)(2,1)S(1)} all-gather(bf16[128,782]{0,1:T(8,128)(2,1)} %param.2), channel_id=1, replica_groups=mesh['row'=8,'col'=4] {'col'}, dimensions={0}, use_global_device_ids=true | all-gather | bytes 1000960 | tf_op jit(solution)/shard_map/all_gather | solution.py:29
  31.3 2.9 slice.304
  34.2 2.8 slice.305
  37.1 2.8 slice.306
  48.4 2.9 slice.310
  51.2 2.9 slice.311
  54.1 2.9 slice.312
  57.0 2.9 slice.313
  68.9 15.6 %fusion.37 = (f32[512]{0:T(512)S(1)}, f32[512,384]{0,1:T(8,128)S(1)}) fusion(f32[512,384]{0,1:T(8,128)} %slice.314, f32[]{:T(128)} %bitcast.15, f32[512,384]{0,1:T(8,128)} %slice.313, f32[]{:T(128)} %bitcast.14, f32[512,384]{0,1:T(8,128)} %slice.312, f32[]{:T(128)} %bitcast.13, f32[512,384]{0,1:T(8,128)} %slice.311, f32[]{:T(128)} %bitcast.12, ...), kind=kLoop, calls=%fused_computation.88 | loop fusion | flops 6290944 | bytes 13371456 | tf_op jit(solution)/shard_map/reduce_sum | solution.py:20
  88.7 4.3 %slice.290 = f32[1024,384]{0,1:T(8,128)} slice(f32[1024,782]{0,1:T(8,128)S(1)} %maximum_convert_fusion), slice={[0:1024:1], [15:782:2]} | slice | bytes 3145728 | tf_op jit(solution)/shard_map/slice | solution.py:19
  93.0 4.3 %slice.288 = f32[1024,384]{0,1:T(8,128)} slice(f32[1024,782]{0,1:T(8,128)S(1)} %maximum_convert_fusion), slice={[0:1024:1], [14:781:2]} | slice | bytes 3145728 | tf_op jit(solution)/shard_map/slice | solution.py:19
  97.3 4.3 %slice.286 = f32[1024,384]{0,1:T(8,128)} slice(f32[1024,782]{0,1:T(8,128)S(1)} %maximum_convert_fusion), slice={[0:1024:1], [13:780:2]} | slice | bytes 3145728 | tf_op jit(solution)/shard_map/slice | solution.py:19
  101.6 4.3 %slice.284 = f32[1024,384]{0,1:T(8,128)} slice(f32[1024,782]{0,1:T(8,128)S(1)} %maximum_convert_fusion), slice={[0:1024:1], [12:779:2]} | slice | bytes 3145728 | tf_op jit(solution)/shard_map/slice | solution.py:19
  105.9 4.4 %slice.282 = f32[1024,384]{0,1:T(8,128)} slice(f32[1024,782]{0,1:T(8,128)S(1)} %maximum_convert_fusion), slice={[0:1024:1], [11:778:2]} | slice | bytes 3145728 | tf_op jit(solution)/shard_map/slice | solution.py:19
  110.2 4.3 %slice.280 = f32[1024,384]{0,1:T(8,128)} slice(f32[1024,782]{0,1:T(8,128)S(1)} %maximum_convert_fusion), slice={[0:1024:1], [10:777:2]} | slice | bytes 3145728 | tf_op jit(solution)/shard_map/slice | solution.py:19
  114.5 4.3 %slice.278 = f32[1024,384]{0,1:T(8,128)} slice(f32[1024,782]{0,1:T(8,128)S(1)} %maximum_convert_fusion), slice={[0:1024:1], [9:776:2]} | slice | bytes 3145728 | tf_op jit(solution)/shard_map/slice | solution.py:19
  118.8 4.2 %slice.276 = f32[1024,384]{0,1:T(8,128)} slice(f32[1024,782]{0,1:T(8,128)S(1)} %maximum_convert_fusion), slice={[0:1024:1], [8:775:2]} | slice | bytes 3145728 | tf_op jit(solution)/shard_map/slice | solution.py:19
  123.0 4.3 %slice.274 = f32[1024,384]{0,1:T(8,128)} slice(f32[1024,782]{0,1:T(8,128)S(1)} %maximum_convert_fusion), slice={[0:1024:1], [7:774:2]} | slice | bytes 3145728 | tf_op jit(solution)/shard_map/slice | solution.py:19
  127.3 4.3 %slice.272 = f32[1024,384]{0,1:T(8,128)} slice(f32[1024,782]{0,1:T(8,128)S(1)} %maximum_convert_fusion), slice={[0:1024:1], [6:773:2]} | slice | bytes 3145728 | tf_op jit(solution)/shard_map/slice | solution.py:19
  131.6 4.3 %slice.270 = f32[1024,384]{0,1:T(8,128)} slice(f32[1024,782]{0,1:T(8,128)S(1)} %maximum_convert_fusion), slice={[0:1024:1], [5:772:2]} | slice | bytes 3145728 | tf_op jit(solution)/shard_map/slice | solution.py:19
  135.9 4.3 %slice.268 = f32[1024,384]{0,1:T(8,128)} slice(f32[1024,782]{0,1:T(8,128)S(1)} %maximum_convert_fusion), slice={[0:1024:1], [4:771:2]} | slice | bytes 3145728 | tf_op jit(solution)/shard_map/slice | solution.py:19
  140.2 4.3 %slice.266 = f32[1024,384]{0,1:T(8,128)} slice(f32[1024,782]{0,1:T(8,128)S(1)} %maximum_convert_fusion), slice={[0:1024:1], [3:770:2]} | slice | bytes 3145728 | tf_op jit(solution)/shard_map/slice | solution.py:19
  144.6 4.3 %slice.264 = f32[1024,384]{0,1:T(8,128)} slice(f32[1024,782]{0,1:T(8,128)S(1)} %maximum_convert_fusion), slice={[0:1024:1], [2:769:2]} | slice | bytes 3145728 | tf_op jit(solution)/shard_map/slice | solution.py:19
  148.9 4.2 %slice.262 = f32[1024,384]{0,1:T(8,128)} slice(f32[1024,782]{0,1:T(8,128)S(1)} %maximum_convert_fusion), slice={[0:1024:1], [1:768:2]} | slice | bytes 3145728 | tf_op jit(solution)/shard_map/slice | solution.py:19
  153.1 4.2 %slice.260 = f32[1024,384]{0,1:T(8,128)} slice(f32[1024,782]{0,1:T(8,128)S(1)} %maximum_convert_fusion), slice={[0:1024:1], [0:767:2]} | slice | bytes 3145728 | tf_op jit(solution)/shard_map/slice | solution.py:19
  157.3 21.6 %fusion.38 = (f32[1024]{0:T(1024)S(1)}, f32[1024,384]{0,1:T(8,128)S(1)}) fusion(f32[1024,384]{0,1:T(8,128)} %slice.290, f32[]{:T(128)} %bitcast.15, f32[1024,384]{0,1:T(8,128)} %slice.288, f32[]{:T(128)} %bitcast.14, f32[1024,384]{0,1:T(8,128)} %slice.286, f32[]{:T(128)} %bitcast.13, f32[1024,384]{0,1:T(8,128)} %slice.284, f32[]{:T(128)} %bitcast.12, ...), kind=kLoop, calls=%fused_computation.89 | loop fusion | flops 12581888 | bytes 26742848 | tf_op jit(solution)/shard_map/reduce_sum | solution.py:20
  187.7 5.1 %multiply_bitcast_fusion.3 = f32[8,512,1024]{1,2,0:T(8,128)S(1)} fusion(bf16[8,1024,353]{1,2,0:T(8,128)(2,1)S(1)} %get-tuple-element.15, bf16[512,353]{0,1:T(8,128)(2,1)S(1)} %copy-done.3), kind=kOutput, calls=%fused_computation.4 | convolution fusion | flops 2965372928 | bytes 22922240 | tf_op jit(solution)/shard_map/in,ljn->lij/dot_general | solution.py:43
  192.8 9.0 %multiply_bitcast_fusion = f32[8,512,1024]{1,2,0:T(8,128)} fusion(bf16[8,1024,353]{1,2,0:T(8,128)(2,1)S(1)} %get-tuple-element.16, bf16[512,353]{0,1:T(8,128)(2,1)S(1)} %copy-done.3), kind=kOutput, calls=%fused_computation.1 | convolution fusion | flops 2965372928 | bytes 22922240 | tf_op jit(solution)/shard_map/in,ljn->lij/dot_general | solution.py:43
  201.9 8.5 %multiply_bitcast_fusion.1 = f32[8,512,1024]{1,2,0:T(8,128)} fusion(bf16[8,1024,353]{1,2,0:T(8,128)(2,1)S(1)} %copy-done.1, bf16[512,353]{0,1:T(8,128)(2,1)S(1)} %copy-done.3), kind=kOutput, calls=%fused_computation.2 | convolution fusion | flops 2965372928 | bytes 22922240 | tf_op jit(solution)/shard_map/in,ljn->lij/dot_general | solution.py:43
  210.4 8.5 %multiply_bitcast_fusion.2 = f32[8,512,1024]{1,2,0:T(8,128)} fusion(bf16[8,1024,353]{1,2,0:T(8,128)(2,1)S(1)} %bitcast.166, bf16[512,353]{0,1:T(8,128)(2,1)S(1)} %copy-done.3), kind=kOutput, calls=%fused_computation.3 | convolution fusion | flops 2965372928 | bytes 22922240 | tf_op jit(solution)/shard_map/in,ljn->lij/dot_general | solution.py:43
  218.8 40.9 %pad_maximum_fusion = f32[32,512,1024]{1,2,0:T(8,128)} fusion(f32[8,512,1024]{1,2,0:T(8,128)} %multiply_bitcast_fusion, f32[8,512,1024]{1,2,0:T(8,128)} %multiply_bitcast_fusion.1, f32[8,512,1024]{1,2,0:T(8,128)} %multiply_bitcast_fusion.2, f32[8,512,1024]{1,2,0:T(8,128)S(1)} %multiply_bitcast_fusion.3), kind=kLoop, calls=%fused_computation | loop fusion | flops 50331648 | bytes 134217728 | tf_op jit(solution)/shard_map/concatenate | solution.py:45
  259.7 65.8 %copy.3 = f32[32,512,1024]{2,1,0:T(8,128)} copy(f32[32,512,1024]{1,2,0:T(8,128)} %pad_maximum_fusion) | data formatting | bytes 134217728 | tf_op jit(solution)/shard_map/concatenate | solution.py:45
  (46 shorter events, 34.3 us)
Async XLA Ops:
  6.5 80.3 %all-reduce.3.cloned.1.call-start = ((), (), s32[]{:S(2)}) async-start(), calls=%async_computation | async-start | bytes 3211264 | tf_op jit(solution)/shard_map/psum | solution.py:12
  48.4 19.8 %copy-start.4 = (f32[16]{0:T(128)S(1)}, f32[16]{0:T(128)}, u32[]{:S(2)}) copy-start(f32[16]{0:T(128)} %param.3) | copy-start | bytes 196
  181.7 5.9 %copy-start.3 = (bf16[512,353]{0,1:T(8,128)(2,1)S(1)}, bf16[512,353]{0,1:T(8,128)(2,1)}, u32[]{:S(2)}) copy-start(bf16[512,353]{0,1:T(8,128)(2,1)} %fusion.24) | copy-start | bytes 1084420
  182.5 2.6 copy-start
  185.1 2.5 copy-start.2
  192.8 9.1 %copy-start.1 = (bf16[8,1024,353]{1,2,0:T(8,128)(2,1)S(1)}, bf16[8,1024,353]{1,2,0:T(8,128)(2,1)}, u32[]{:S(2)}) copy-start(bf16[8,1024,353]{1,2,0:T(8,128)(2,1)} %copy-done) | copy-start | bytes 17350660
  192.8 17.5 %slice-start = ((s8[5898240]{0:T(1024)(128)(4,1)}), s8[1703936]{0:T(1024)(128)(4,1)S(1)}, s32[]{:S(2)}) async-start(s8[5898240]{0:T(1024)(128)(4,1)} %bitcast.165), calls=%async_computation.1 | async-start | bytes 3407872
  201.9 8.5 %slice-start.1 = ((s8[5898240]{0:T(1024)(128)(4,1)}), s8[4194304]{0:T(1024)(128)(4,1)S(1)}, s32[]{:S(2)}) async-start(s8[5898240]{0:T(1024)(128)(4,1)} %bitcast.165), calls=%async_computation.2 | async-start | bytes 8388608
Sparse Core Ops, SparseCore 0:
  28.8 58.0 all-reduce.2
where the time goes:
time: 334 us; the launch traced here: 332 us
  local copies, waits for them, and re-layouts  183 us (55%)
  other arithmetic  82.7 us (25%)
  matrix products  31.1 us (9%)
  blocking collectives  20.8 us (6%)
  between operations  13.6 us (4%)
    slice x33, local copies, waits for them, and re-layouts, whiten(): decimated = decimated + taps[k] * samples[:, k:k + 2 * count - 1:2]  109 us
    concatenate x1, local copies, waits for them, and re-layouts, on_device(): return jnp.concatenate(groups, axis=0)  65.8 us
    concatenate x1, other arithmetic, on_device(): return jnp.concatenate(groups, axis=0)  40.9 us
    reduce_sum x2, other arithmetic, whiten(): centred = decimated - jnp.mean(decimated, axis=1, keepdims=True)  37.2 us
    dot_general x4, matrix products, on_device(): jnp.einsum('in,ljn->lij', left, shifted, preferred_element_type=jnp.float32)  31.1 us
    all_gather x1, blocking collectives, on_device(): source = lax.all_gather(traces, 'col', axis=0, tiled=True)  20.8 us
    unnamed x21, local copies, waits for them, and re-layouts  7.78 us
  transfers between devices with their start and end apart: 1, of which 1 were waited for; matrix products, arithmetic and copies ran while one was open for 17% of the time, Pallas kernels for 0%

commit v1 on v0

--- a/solution.py
+++ b/solution.py
@@ -26,7 +26,27 @@
     count = (traces.shape[1] - taps.shape[0] + 2) // 2
     factor = lax.axis_size("row") // lax.axis_size("col")
     column = lax.axis_index("col")
-    source = lax.all_gather(traces, "col", axis=0, tiled=True)
+    prior, formed, front = (lax.axis_size("col"), lax.axis_index("col"), traces.shape[0])
+    runs = []
+    for to_i in range(prior):
+        runs.append((to_i, (to_i + 1) % prior))
+    queue = []
+    for to_i in range(prior):
+        queue.append((to_i, (to_i - 1) % prior))
+    source = jnp.zeros((*traces.shape[:0], prior * front, *traces.shape[0 + 1 :]), traces.dtype)
+    source = lax.dynamic_update_slice_in_dim(source, traces, formed * front, axis=0)
+    row_out = val = traces
+    inter = prior // 2
+    for w in range(1, inter + 1):
+        row_out = lax.ppermute(row_out, "col", runs)
+        source = lax.dynamic_update_slice_in_dim(
+            source, row_out, (formed - w) % prior * front, axis=0
+        )
+        if w < prior - inter:
+            val = lax.ppermute(val, "col", queue)
+            source = lax.dynamic_update_slice_in_dim(
+                source, val, (formed + w) % prior * front, axis=0
+            )
     first_block = whiten(source, taps, count)
     pieces = [from_root(source, "row", factor * column + k) for k in range(factor)]
     second_block = jnp.concatenate(pieces, axis=0)

time: 334 us -> 374 us (1.12)
  waiting for transfers between devices: 1.4 us -> 53.7 us
  blocking collectives: 20.8 us -> 0 us
  starting transfers between devices: 0.01 us -> 6.68 us
    psum x1, waiting for transfers between devices: 1.39 us -> 41.2 us  [from_root(): return lax.psum(jnp.where(mine, array, jnp.zeros_like(array)), axis)]
    all_gather x1 -> x0, blocking collectives: 20.8 us -> none  [on_device(): source = lax.all_gather(traces, 'col', axis=0, tiled=True)]
    ppermute x0 -> x3, waiting for transfers between devices: none -> 12.6 us  [the longest x2 12.6 us: on_device(): row_out = lax.ppermute(row_out, 'col', runs)]
    ppermute x0 -> x3, starting transfers between devices: none -> 6.67 us  [the longest x1 5.05 us: on_device(): val = lax.ppermute(val, 'col', queue)]
    unnamed x21 -> x19, local copies, waits for them, and re-layouts: 7.78 us -> 7.78 us
  transfers between devices with their start and end apart: 1 -> 4, of which waited for: 1 -> 3; matrix products, arithmetic and copies ran while one was open for 17% -> 5% of each run, Pallas kernels for 0% -> 0%
where the time goes in v1:
time: 374 us; the launch traced here: 373 us
  local copies, waits for them, and re-layouts  185 us (49%)
  other arithmetic  82.6 us (22%)
  waiting for transfers between devices  53.7 us (14%)
  matrix products  31.2 us (8%)
  between operations  13.6 us (4%)
  starting transfers between devices  6.68 us (2%)
    slice x33, local copies, waits for them, and re-layouts, whiten(): decimated = decimated + taps[k] * samples[:, k:k + 2 * count - 1:2]  110 us
    concatenate x1, local copies, waits for them, and re-layouts, on_device(): return jnp.concatenate(groups, axis=0)  65.8 us
    psum x1, waiting for transfers between devices, from_root(): return lax.psum(jnp.where(mine, array, jnp.zeros_like(array)), axis)  41.2 us
    concatenate x1, other arithmetic, on_device(): return jnp.concatenate(groups, axis=0)  40.9 us
    reduce_sum x2, other arithmetic, whiten(): centred = decimated - jnp.mean(decimated, axis=1, keepdims=True)  37.2 us
    dot_general x4, matrix products, on_device(): jnp.einsum('in,ljn->lij', left, shifted, preferred_element_type=jnp.float32)  31.2 us
    ppermute x2, waiting for transfers between devices, on_device(): row_out = lax.ppermute(row_out, 'col', runs)  12.6 us
    unnamed x19, local copies, waits for them, and re-layouts  7.78 us
  transfers between devices with their start and end apart: 4, of which 3 were waited for; matrix products, arithmetic and copies ran while one was open for 5% of the time, Pallas kernels for 0%

profile of v1, /device:TPU:0, one launch (start us, length us, event | category | flops | bytes accessed | tf_op | source)
XLA Modules:
  0.0 373.0 jit_solution(14233011276068738594)
XLA Ops:
  6.5 5.0 %collective-permute-start.1 = (bf16[128,782]{0,1:T(8,128)(2,1)}, bf16[128,782]{0,1:T(8,128)(2,1)S(1)}, u32[]{:S(2)}, u32[]{:S(2)}) collective-permute-start(bf16[128,782]{0,1:T(8,128)(2,1)} %param.2), channel_id=1, source_target_pairs={{0,3},{1,0},{2,1},{3,2},{4,7},{5,4},{6,5},{7,6},{8,11},{9,8},{10,9... | collective-permute-start | bytes 600584 | tf_op jit(solution)/shard_map/ppermute | solution.py:46
  14.6 6.7 %collective-permute-done = bf16[128,782]{0,1:T(8,128)(2,1)S(1)} collective-permute-done((bf16[128,782]{0,1:T(8,128)(2,1)}, bf16[128,782]{0,1:T(8,128)(2,1)S(1)}, u32[]{:S(2)}, u32[]{:S(2)}) %collective-permute-start) | collective-permute-done | bytes 200224 | tf_op jit(solution)/shard_map/ppermute | solution.py:41
  23.0 5.9 %collective-permute-done.2 = bf16[128,782]{0,1:T(8,128)(2,1)S(1)} collective-permute-done((bf16[128,782]{0,1:T(8,128)(2,1)S(1)}, bf16[128,782]{0,1:T(8,128)(2,1)S(1)}, u32[]{:S(2)}, u32[]{:S(2)}) %collective-permute-start.2) | collective-permute-done | bytes 200224 | tf_op jit(solution)/shard_map/ppermute | solution.py:41
  31.7 2.9 slice.304
  45.8 2.9 slice.309
  48.7 2.9 slice.310
  54.4 2.9 slice.312
  69.7 15.6 %fusion.37 = (f32[512]{0:T(512)S(1)}, f32[512,384]{0,1:T(8,128)S(1)}) fusion(f32[512,384]{0,1:T(8,128)} %slice.314, f32[]{:T(128)} %bitcast.15, f32[512,384]{0,1:T(8,128)} %slice.313, f32[]{:T(128)} %bitcast.14, f32[512,384]{0,1:T(8,128)} %slice.312, f32[]{:T(128)} %bitcast.13, f32[512,384]{0,1:T(8,128)} %slice.311, f32[]{:T(128)} %bitcast.12, ...), kind=kLoop, calls=%fused_computation.92 | loop fusion | flops 6290944 | bytes 13371456 | tf_op jit(solution)/shard_map/reduce_sum | solution.py:20
  86.2 41.2 %all-reduce.3.cloned.1.call-done = (bf16[512,782]{0,1:T(8,128)(2,1)}, bf16[512,782]{0,1:T(8,128)(2,1)}) async-done(((bf16[512,782]{0,1:T(8,128)(2,1)}, bf16[512,782]{0,1:T(8,128)(2,1)}), (bf16[512,782]{0,1:T(8,128)(2,1)}, bf16[512,782]{0,1:T(8,128)(2,1)})) %all-reduce.3.cloned.1.call-update) | async-done | bytes 1601552 | tf_op jit(solution)/shard_map/psum | solution.py:12
  129.2 4.3 %slice.290 = f32[1024,384]{0,1:T(8,128)} slice(f32[1024,782]{0,1:T(8,128)S(1)} %maximum_convert_fusion), slice={[0:1024:1], [15:782:2]} | slice | bytes 3145728 | tf_op jit(solution)/shard_map/slice | solution.py:19
  133.5 4.3 %slice.288 = f32[1024,384]{0,1:T(8,128)} slice(f32[1024,782]{0,1:T(8,128)S(1)} %maximum_convert_fusion), slice={[0:1024:1], [14:781:2]} | slice | bytes 3145728 | tf_op jit(solution)/shard_map/slice | solution.py:19
  137.8 4.3 %slice.286 = f32[1024,384]{0,1:T(8,128)} slice(f32[1024,782]{0,1:T(8,128)S(1)} %maximum_convert_fusion), slice={[0:1024:1], [13:780:2]} | slice | bytes 3145728 | tf_op jit(solution)/shard_map/slice | solution.py:19
  142.1 4.3 %slice.284 = f32[1024,384]{0,1:T(8,128)} slice(f32[1024,782]{0,1:T(8,128)S(1)} %maximum_convert_fusion), slice={[0:1024:1], [12:779:2]} | slice | bytes 3145728 | tf_op jit(solution)/shard_map/slice | solution.py:19
  146.4 4.4 %slice.282 = f32[1024,384]{0,1:T(8,128)} slice(f32[1024,782]{0,1:T(8,128)S(1)} %maximum_convert_fusion), slice={[0:1024:1], [11:778:2]} | slice | bytes 3145728 | tf_op jit(solution)/shard_map/slice | solution.py:19
  150.8 4.3 %slice.280 = f32[1024,384]{0,1:T(8,128)} slice(f32[1024,782]{0,1:T(8,128)S(1)} %maximum_convert_fusion), slice={[0:1024:1], [10:777:2]} | slice | bytes 3145728 | tf_op jit(solution)/shard_map/slice | solution.py:19
  155.1 4.2 %slice.278 = f32[1024,384]{0,1:T(8,128)} slice(f32[1024,782]{0,1:T(8,128)S(1)} %maximum_convert_fusion), slice={[0:1024:1], [9:776:2]} | slice | bytes 3145728 | tf_op jit(solution)/shard_map/slice | solution.py:19
  159.4 4.2 %slice.276 = f32[1024,384]{0,1:T(8,128)} slice(f32[1024,782]{0,1:T(8,128)S(1)} %maximum_convert_fusion), slice={[0:1024:1], [8:775:2]} | slice | bytes 3145728 | tf_op jit(solution)/shard_map/slice | solution.py:19
  163.6 4.3 %slice.274 = f32[1024,384]{0,1:T(8,128)} slice(f32[1024,782]{0,1:T(8,128)S(1)} %maximum_convert_fusion), slice={[0:1024:1], [7:774:2]} | slice | bytes 3145728 | tf_op jit(solution)/shard_map/slice | solution.py:19
  167.9 4.3 %slice.272 = f32[1024,384]{0,1:T(8,128)} slice(f32[1024,782]{0,1:T(8,128)S(1)} %maximum_convert_fusion), slice={[0:1024:1], [6:773:2]} | slice | bytes 3145728 | tf_op jit(solution)/shard_map/slice | solution.py:19
  172.2 4.3 %slice.270 = f32[1024,384]{0,1:T(8,128)} slice(f32[1024,782]{0,1:T(8,128)S(1)} %maximum_convert_fusion), slice={[0:1024:1], [5:772:2]} | slice | bytes 3145728 | tf_op jit(solution)/shard_map/slice | solution.py:19
  176.5 4.3 %slice.268 = f32[1024,384]{0,1:T(8,128)} slice(f32[1024,782]{0,1:T(8,128)S(1)} %maximum_convert_fusion), slice={[0:1024:1], [4:771:2]} | slice | bytes 3145728 | tf_op jit(solution)/shard_map/slice | solution.py:19
  180.8 4.3 %slice.266 = f32[1024,384]{0,1:T(8,128)} slice(f32[1024,782]{0,1:T(8,128)S(1)} %maximum_convert_fusion), slice={[0:1024:1], [3:770:2]} | slice | bytes 3145728 | tf_op jit(solution)/shard_map/slice | solution.py:19
  185.2 4.3 %slice.264 = f32[1024,384]{0,1:T(8,128)} slice(f32[1024,782]{0,1:T(8,128)S(1)} %maximum_convert_fusion), slice={[0:1024:1], [2:769:2]} | slice | bytes 3145728 | tf_op jit(solution)/shard_map/slice | solution.py:19
  189.5 4.2 %slice.262 = f32[1024,384]{0,1:T(8,128)} slice(f32[1024,782]{0,1:T(8,128)S(1)} %maximum_convert_fusion), slice={[0:1024:1], [1:768:2]} | slice | bytes 3145728 | tf_op jit(solution)/shard_map/slice | solution.py:19
  193.7 4.2 %slice.260 = f32[1024,384]{0,1:T(8,128)} slice(f32[1024,782]{0,1:T(8,128)S(1)} %maximum_convert_fusion), slice={[0:1024:1], [0:767:2]} | slice | bytes 3145728 | tf_op jit(solution)/shard_map/slice | solution.py:19
  197.9 21.6 %fusion.38 = (f32[1024]{0:T(1024)S(1)}, f32[1024,384]{0,1:T(8,128)S(1)}) fusion(f32[1024,384]{0,1:T(8,128)} %slice.290, f32[]{:T(128)} %bitcast.15, f32[1024,384]{0,1:T(8,128)} %slice.288, f32[]{:T(128)} %bitcast.14, f32[1024,384]{0,1:T(8,128)} %slice.286, f32[]{:T(128)} %bitcast.13, f32[1024,384]{0,1:T(8,128)} %slice.284, f32[]{:T(128)} %bitcast.12, ...), kind=kLoop, calls=%fused_computation.93 | loop fusion | flops 12581888 | bytes 26742848 | tf_op jit(solution)/shard_map/reduce_sum | solution.py:20
  228.3 5.1 %multiply_bitcast_fusion.3 = f32[8,512,1024]{1,2,0:T(8,128)S(1)} fusion(bf16[8,1024,353]{1,2,0:T(8,128)(2,1)S(1)} %get-tuple-element.15, bf16[512,353]{0,1:T(8,128)(2,1)S(1)} %copy-done.3), kind=kOutput, calls=%fused_computation.4 | convolution fusion | flops 2965372928 | bytes 22922240 | tf_op jit(solution)/shard_map/in,ljn->lij/dot_general | solution.py:63
  233.4 9.0 %multiply_bitcast_fusion = f32[8,512,1024]{1,2,0:T(8,128)} fusion(bf16[8,1024,353]{1,2,0:T(8,128)(2,1)S(1)} %get-tuple-element.16, bf16[512,353]{0,1:T(8,128)(2,1)S(1)} %copy-done.3), kind=kOutput, calls=%fused_computation.1 | convolution fusion | flops 2965372928 | bytes 22922240 | tf_op jit(solution)/shard_map/in,ljn->lij/dot_general | solution.py:63
  242.5 8.5 %multiply_bitcast_fusion.1 = f32[8,512,1024]{1,2,0:T(8,128)} fusion(bf16[8,1024,353]{1,2,0:T(8,128)(2,1)S(1)} %copy-done.1, bf16[512,353]{0,1:T(8,128)(2,1)S(1)} %copy-done.3), kind=kOutput, calls=%fused_computation.2 | convolution fusion | flops 2965372928 | bytes 22922240 | tf_op jit(solution)/shard_map/in,ljn->lij/dot_general | solution.py:63
  251.0 8.5 %multiply_bitcast_fusion.2 = f32[8,512,1024]{1,2,0:T(8,128)} fusion(bf16[8,1024,353]{1,2,0:T(8,128)(2,1)S(1)} %bitcast.166, bf16[512,353]{0,1:T(8,128)(2,1)S(1)} %copy-done.3), kind=kOutput, calls=%fused_computation.3 | convolution fusion | flops 2965372928 | bytes 22922240 | tf_op jit(solution)/shard_map/in,ljn->lij/dot_general | solution.py:63
  259.5 40.9 %pad_maximum_fusion = f32[32,512,1024]{1,2,0:T(8,128)} fusion(f32[8,512,1024]{1,2,0:T(8,128)} %multiply_bitcast_fusion, f32[8,512,1024]{1,2,0:T(8,128)} %multiply_bitcast_fusion.1, f32[8,512,1024]{1,2,0:T(8,128)} %multiply_bitcast_fusion.2, f32[8,512,1024]{1,2,0:T(8,128)S(1)} %multiply_bitcast_fusion.3), kind=kLoop, calls=%fused_computation | loop fusion | flops 50331648 | bytes 134217728 | tf_op jit(solution)/shard_map/concatenate | solution.py:65
  300.4 65.8 %copy.3 = f32[32,512,1024]{2,1,0:T(8,128)} copy(f32[32,512,1024]{1,2,0:T(8,128)} %pad_maximum_fusion) | data formatting | bytes 134217728 | tf_op jit(solution)/shard_map/concatenate | solution.py:65
  (54 shorter events, 45.4 us)
Async XLA Ops:
  6.5 120.9 %all-reduce.3.cloned.1.call-start = ((), (), s32[]{:S(2)}) async-start(), calls=%async_computation | async-start | bytes 3211264 | tf_op jit(solution)/shard_map/psum | solution.py:12
  6.5 16.4 %collective-permute-start.1 = (bf16[128,782]{0,1:T(8,128)(2,1)}, bf16[128,782]{0,1:T(8,128)(2,1)S(1)}, u32[]{:S(2)}, u32[]{:S(2)}) collective-permute-start(bf16[128,782]{0,1:T(8,128)(2,1)} %param.2), channel_id=1, source_target_pairs={{0,3},{1,0},{2,1},{3,2},{4,7},{5,4},{6,5},{7,6},{8,11},{9,8},{10,9... | collective-permute-start | bytes 600584 | tf_op jit(solution)/shard_map/ppermute | solution.py:46
  11.6 9.7 %collective-permute-start = (bf16[128,782]{0,1:T(8,128)(2,1)}, bf16[128,782]{0,1:T(8,128)(2,1)S(1)}, u32[]{:S(2)}, u32[]{:S(2)}) collective-permute-start(bf16[128,782]{0,1:T(8,128)(2,1)} %param.2), channel_id=1, source_target_pairs={{0,1},{1,2},{2,3},{3,0},{4,5},{5,6},{6,7},{7,4},{8,9},{9,10},{10,1... | collective-permute-start | bytes 600584 | tf_op jit(solution)/shard_map/ppermute | solution.py:41
  21.3 7.7 %collective-permute-start.2 = (bf16[128,782]{0,1:T(8,128)(2,1)S(1)}, bf16[128,782]{0,1:T(8,128)(2,1)S(1)}, u32[]{:S(2)}, u32[]{:S(2)}) collective-permute-start(bf16[128,782]{0,1:T(8,128)(2,1)S(1)} %collective-permute-done), channel_id=1, source_target_pairs={{0,1},{1,2},{2,3},{3,0},{4,5},{5,6},{6,7},{7,4},{8,9},{9,10},{10,1... | collective-permute-start | bytes 600584 | tf_op jit(solution)/shard_map/ppermute | solution.py:41
  222.4 5.9 %copy-start.3 = (bf16[512,353]{0,1:T(8,128)(2,1)S(1)}, bf16[512,353]{0,1:T(8,128)(2,1)}, u32[]{:S(2)}) copy-start(bf16[512,353]{0,1:T(8,128)(2,1)} %fusion.24) | copy-start | bytes 1084420
  223.2 2.6 copy-start
  225.7 2.5 copy-start.2
  233.4 9.1 %copy-start.1 = (bf16[8,1024,353]{1,2,0:T(8,128)(2,1)S(1)}, bf16[8,1024,353]{1,2,0:T(8,128)(2,1)}, u32[]{:S(2)}) copy-start(bf16[8,1024,353]{1,2,0:T(8,128)(2,1)} %copy-done) | copy-start | bytes 17350660
  233.4 17.5 %slice-start = ((s8[5898240]{0:T(1024)(128)(4,1)}), s8[1703936]{0:T(1024)(128)(4,1)S(1)}, s32[]{:S(2)}) async-start(s8[5898240]{0:T(1024)(128)(4,1)} %bitcast.165), calls=%async_computation.1 | async-start | bytes 3407872
  242.5 8.5 %slice-start.1 = ((s8[5898240]{0:T(1024)(128)(4,1)}), s8[4194304]{0:T(1024)(128)(4,1)S(1)}, s32[]{:S(2)}) async-start(s8[5898240]{0:T(1024)(128)(4,1)} %bitcast.165), calls=%async_computation.2 | async-start | bytes 8388608
Sparse Core Ops, SparseCore 0:
  69.8 57.5 all-reduce.2
